TPU v7x, 256 devices: a whole 4x4x8 slice. The times are simulated.
256 devices in a mesh: ctx: 16 (over y, x), head: 8 (over z), batch: 2 (over core).
Axes of the slice: x: 4, y: 4, z: 8, core: 2. Of those that a mesh axis runs over, the one named last changes fastest.
Arguments:
- queries: bfloat16 [4096, 16384], P(('batch', 'ctx'), 'head'), parts along dimension 0, may hold values from -6 to 6
- new_keys: bfloat16 [4096, 1024], P(('batch', 'ctx'), 'head'), parts along dimension 0, may hold values from -6 to 6
- new_values: bfloat16 [4096, 1024], P(('batch', 'ctx'), 'head'), parts along dimension 0, may hold values from -6 to 6
- cache_keys: bfloat16 [16384, 1024], P(('batch', 'ctx'), 'head'), parts along dimension 0, may hold values from -6 to 6
- cache_values: bfloat16 [16384, 1024], P(('batch', 'ctx'), 'head'), parts along dimension 0, may hold values from -6 to 6
- cache_lens: int32 [32], P('batch'), parts along dimension 0, may hold values from 1 to 512, 5120 in all
- new_pos: int32 [4096], P('batch'), parts along dimension 0, may hold values from 0 to 2047, each once
Outputs:
- attended: bfloat16 [4096, 16384], P(('batch', 'ctx'), 'head'), parts along dimension 0
There are 2 independent parts, one for each index of `batch`. A program takes and returns all parts, laid end to end along the dimension named above; each array names one. Nothing has to cross between parts.
Inputs may be any that keep to these rules, and one draw needn't show every extreme that they name: `cache_lens`: every block holds at least one filled slot, and in every request some block is full with 512. `new_pos`: each position appears once.
All inputs are finite; a program needn't handle non-finite values.
Results may differ from a plain program's by a relative error of at most 0.0055.
Values may be sent and summed in bfloat16 or wider, within the bound.
No kernel may reach another device: no remote copies, remote signals or barrier semaphores. Data moves between devices by JAX's collectives and lax.ppermute only.
A program may use at most 128 MiB of HBM per device.

v0:
```python
import functools
import jax
import jax.numpy as jnp
from jax import lax
from jax.experimental import pallas as pl
from jax.experimental.pallas import tpu as pltpu
from jax.sharding import PartitionSpec as P

HD = 128
SIDE = 4
HG = 4
NEG = -1e30
LIMIT = 1e37
VMEM = 40 * 2**20
LOG2E = 1.4426950408889634

OWN = ((0, 0),)
NEAR = ((0, -1), (0, 1), (-1, 0), (1, 0))
FAR = ((0, 2), (2, 0))
DIAG = ((-1, -1), (1, -1), (-1, 1), (1, 1))
REST = ((2, -1), (2, 1), (-1, 2), (1, 2), (2, 2))
ORDER = OWN + NEAR + FAR + DIAG + REST


def from_offset(block, dy, dx):
    route = []
    for y in range(SIDE):
        for x in range(SIDE):
            route.append((((y + dy) % SIDE) * SIDE + (x + dx) % SIDE, y * SIDE + x))
    return lax.ppermute(block, "ctx", route)


def rows_of(q_ref):
    return jnp.concatenate([q_ref[:, i * HD:(i + 1) * HD] for i in range(HG)], 0)


def own_columns(pos_ref, me, tokens):
    row = pos_ref[pl.ds(me, 1), :]
    return jnp.broadcast_to(row, (tokens, tokens)).T


def prepare(kv_refs, src_ref, lens_ref, pos_ref, kt_ref, va_ref, mask_ref, first, cached, tokens):
    width = cached + tokens
    own = own_columns(pos_ref, src_ref[0], tokens)
    slot = 0
    for ref in kv_refs:
        for part in range(ref.shape[0] // (2 * width)):
            base = part * 2 * width
            source = src_ref[first + slot]
            kt_ref[:, slot * width:(slot + 1) * width] = ref[base:base + width, :].T
            valid = lax.broadcasted_iota(jnp.int32, (cached, HD), 0) < lens_ref[source]
            stored = ref[base + width:base + width + cached, :]
            at = slot * width
            va_ref[at:at + cached, :HD] = jnp.where(valid, stored, jnp.zeros_like(stored))
            va_ref[at:at + cached, HD:] = jnp.where(valid, 1.0, 0.0).astype(jnp.bfloat16)
            va_ref[at + cached:at + width, :HD] = ref[base + width + cached:base + 2 * width, :]
            va_ref[at + cached:at + width, HD:] = jnp.ones((tokens, HD), jnp.bfloat16)
            seen = pos_ref[pl.ds(source, 1), :] <= own
            mask_ref[slot] = jnp.where(seen, 1.0, 0.0).astype(jnp.bfloat16)
            slot += 1
    return slot


def first_kernel(src_ref, lens_ref, q_ref, pos_ref, kv_ref, acc_ref, m_ref, kt_ref, va_ref, mask_ref, *, cached, tokens):
    @pl.when(pl.program_id(0) == 0)
    def _():
        prepare([kv_ref], src_ref, lens_ref, pos_ref, kt_ref, va_ref, mask_ref, 0, cached, tokens)

    scale = LOG2E * HD ** -0.5
    q = rows_of(q_ref)
    scores = jnp.dot(q, kt_ref[...], preferred_element_type=jnp.float32) * scale
    lane = lax.broadcasted_iota(jnp.int32, (1, cached), 1)
    bias = jnp.where(lane < lens_ref[src_ref[0]], 0.0, NEG)
    shown = jnp.concatenate([mask_ref[0].astype(jnp.float32)] * HG, 0) > 0.5
    scores = jnp.concatenate([scores[:, :cached] + bias, jnp.where(shown, scores[:, cached:], NEG)], 1)
    peak = jnp.max(scores, 1, keepdims=True)
    weights = jnp.exp2(scores - peak).astype(jnp.bfloat16)
    acc_ref[...] = jnp.dot(weights, va_ref[...], preferred_element_type=jnp.float32)
    for i in range(HG):
        m_ref[0, :, i:i + 1] = peak[i * tokens:(i + 1) * tokens, :]


def add_blocks(q_ref, m_ref, acc, kt_ref, va_ref, mask_ref, blocks, cached, tokens):
    width = cached + tokens
    scale = LOG2E * HD ** -0.5
    q = rows_of(q_ref)
    peak = jnp.concatenate([m_ref[0, :, i:i + 1] for i in range(HG)], 0)
    for b in range(blocks):
        at = b * width
        scores = jnp.dot(q, kt_ref[:, at:at + width], preferred_element_type=jnp.float32)
        weights = jnp.exp2(scores * scale - peak).astype(jnp.bfloat16)
        seen = jnp.concatenate([mask_ref[b]] * HG, 0)
        weights = jnp.concatenate([weights[:, :cached], weights[:, cached:] * seen], 1)
        acc = acc + jnp.dot(weights, va_ref[at:at + width, :], preferred_element_type=jnp.float32)
    return acc


def middle_kernel(src_ref, lens_ref, q_ref, pos_ref, m_ref, acc_in, *refs, first, count, cached, tokens):
    kv_refs, (acc_out, kt_ref, va_ref, mask_ref) = refs[:-4], refs[-4:]

    @pl.when(pl.program_id(0) == 0)
    def _():
        prepare(kv_refs, src_ref, lens_ref, pos_ref, kt_ref, va_ref, mask_ref, first, cached, tokens)

    acc_out[...] = add_blocks(q_ref, m_ref, acc_in[...], kt_ref, va_ref, mask_ref, count, cached, tokens)


def safe_rows(q_ref, acc_ref, peak_ref, everything, all_ref, sem, src_ref, lens_ref, pos_ref, cached, tokens):
    width = cached + tokens
    scale = LOG2E * HD ** -0.5
    slot = 0
    for ref in everything:
        for part in range(ref.shape[0] // (2 * width)):
            copy = pltpu.make_async_copy(ref.at[pl.ds(part * 2 * width, 2 * width)], all_ref.at[slot], sem)
            copy.start()
            copy.wait()
            slot += 1
    own = own_columns(pos_ref, src_ref[0], tokens)
    q = rows_of(q_ref)
    peak_ref[...] = jnp.full(peak_ref.shape, NEG, jnp.float32)
    acc_ref[...] = jnp.zeros(acc_ref.shape, jnp.float32)

    def step(b, carry):
        source = src_ref[b]
        scores = lax.dot_general(
            q, all_ref[b, :width, :], (((1,), (1,)), ((), ())), preferred_element_type=jnp.float32
        ) * scale
        lane = lax.broadcasted_iota(jnp.int32, (tokens, cached), 1)
        filled = jnp.where(lane < lens_ref[source], 1.0, 0.0)
        seen = jnp.where(pos_ref[pl.ds(source, 1), :] <= own, 1.0, 0.0)
        shown = jnp.concatenate([jnp.concatenate([filled, seen], 1)] * HG, 0) > 0.5
        scores = jnp.where(shown, scores, NEG)
        old = peak_ref[...]
        new = jnp.maximum(old, jnp.max(scores, 1, keepdims=True))
        weights = jnp.where(shown, jnp.exp2(scores - new[:, :1]), 0.0).astype(jnp.bfloat16)
        values = jnp.concatenate([all_ref[b, width:, :], jnp.ones((width, HD), jnp.bfloat16)], 1)
        factor = jnp.exp2(old - new)
        acc_ref[...] = acc_ref[...] * factor[:, :1] + jnp.dot(weights, values, preferred_element_type=jnp.float32)
        peak_ref[...] = new
        return carry

    lax.fori_loop(0, SIDE * SIDE, step, 0)


def last_kernel(src_ref, lens_ref, q_ref, pos_ref, m_ref, acc_in, *refs, first, count, parts, others, cached, tokens):
    kv_refs, others_refs = refs[:parts], refs[parts:parts + others]
    out_ref, kt_ref, va_ref, mask_ref, acc_ref, peak_ref, all_ref, sem = refs[parts + others:]

    @pl.when(pl.program_id(0) == 0)
    def _():
        prepare(kv_refs, src_ref, lens_ref, pos_ref, kt_ref, va_ref, mask_ref, first, cached, tokens)

    def finish(acc):
        result = (acc[:, :HD] / acc[:, HD:]).astype(jnp.bfloat16)
        for i in range(HG):
            out_ref[:, i * HD:(i + 1) * HD] = result[i * tokens:(i + 1) * tokens, :]

    acc = add_blocks(q_ref, m_ref, acc_in[...], kt_ref, va_ref, mask_ref, count, cached, tokens)
    finish(acc)
    bad = jnp.max(jnp.where(acc[:, HD:] < LIMIT, 0.0, 1.0)) > 0.5

    @pl.when(bad)
    def _():
        safe_rows(q_ref, acc_ref, peak_ref, others_refs, all_ref, sem, src_ref, lens_ref, pos_ref, cached, tokens)
        finish(acc_ref[...])


def shards(queries, new_keys, new_values, cache_keys, cache_values, cache_lens, new_pos):
    here = lax.axis_index("ctx")
    tokens, cached = new_keys.shape[0], cache_keys.shape[0]
    width = cached + tokens
    groups = queries.shape[1] // (HG * HD)
    rows = HG * tokens
    y, x = here // SIDE, here % SIDE
    offsets = jnp.array(ORDER, jnp.int32)
    sources = ((y + offsets[:, 0]) % SIDE) * SIDE + (x + offsets[:, 1]) % SIDE
    positions = new_pos.reshape(-1, tokens)

    smem = pl.BlockSpec(memory_space=pltpu.SMEM)
    whole = pl.BlockSpec(memory_space=pltpu.VMEM)
    head_block = pl.BlockSpec((tokens, HG * HD), lambda g: (0, g))
    acc_block = pl.BlockSpec((rows, 2 * HD), lambda g: (g, 0))
    peak_block = pl.BlockSpec((1, tokens, HD), lambda g: (g, 0, 0))
    acc_shape = jax.ShapeDtypeStruct((groups * rows, 2 * HD), jnp.float32)
    peak_shape = jax.ShapeDtypeStruct((groups, tokens, HD), jnp.float32)
    params = pltpu.CompilerParams(vmem_limit_bytes=VMEM)

    def scratch(blocks):
        return [
            pltpu.VMEM((HD, blocks * width), jnp.bfloat16),
            pltpu.VMEM((blocks * width, 2 * HD), jnp.bfloat16),
            pltpu.VMEM((blocks, tokens, tokens), jnp.bfloat16),
        ]

    def begin(own):
        return pl.pallas_call(
            functools.partial(first_kernel, cached=cached, tokens=tokens),
            grid=(groups,),
            in_specs=[smem, smem, head_block, whole, whole],
            out_specs=[acc_block, peak_block],
            out_shape=[acc_shape, peak_shape],
            scratch_shapes=scratch(1),
            compiler_params=params,
        )(sources, cache_lens, queries, positions, own)

    def add(acc, peak, parts, first, count):
        return pl.pallas_call(
            functools.partial(middle_kernel, first=first, count=count, cached=cached, tokens=tokens),
            grid=(groups,),
            in_specs=[smem, smem, head_block, whole, peak_block, acc_block] + [whole] * len(parts),
            out_specs=acc_block,
            out_shape=acc_shape,
            input_output_aliases={5: 0},
            scratch_shapes=scratch(count),
            compiler_params=params,
        )(sources, cache_lens, queries, positions, peak, acc, *parts)

    def end(acc, peak, parts, first, count, everything):
        return pl.pallas_call(
            functools.partial(last_kernel, first=first, count=count, parts=len(parts), others=len(everything),
                              cached=cached, tokens=tokens),
            grid=(groups,),
            in_specs=[smem, smem, head_block, whole, peak_block, acc_block] + [whole] * len(parts)
            + [whole] * len(everything),
            out_specs=head_block,
            out_shape=jax.ShapeDtypeStruct(queries.shape, jnp.bfloat16),
            scratch_shapes=scratch(count) + [
                pltpu.VMEM((rows, 2 * HD), jnp.float32),
                pltpu.VMEM((rows, HD), jnp.float32),
                pltpu.VMEM((SIDE * SIDE, 2 * width, HD), jnp.bfloat16),
                pltpu.SemaphoreType.DMA,
            ],
            compiler_params=params,
        )(sources, cache_lens, queries, positions, peak, acc, *parts, *everything)

    own = jnp.concatenate([cache_keys, new_keys, cache_values, new_values], 0)
    up, down = from_offset(own, -1, 0), from_offset(own, 1, 0)
    left, right = from_offset(own, 0, -1), from_offset(own, 0, 1)
    over_y, over_x = from_offset(own, 2, 0), from_offset(own, 0, 2)
    acc, peak = begin(own)

    acc, up, down, left, right = lax.optimization_barrier((acc, up, down, left, right))
    column = jnp.concatenate([up, down], 0)
    diag_left, diag_right = from_offset(column, 0, -1), from_offset(column, 0, 1)
    acc = add(acc, peak, [left, right, up, down], 1, 4)

    acc, over_y, over_x = lax.optimization_barrier((acc, over_y, over_x))
    far_left, far_right = from_offset(over_y, 0, -1), from_offset(over_y, 0, 1)
    far_up, far_down = from_offset(over_x, -1, 0), from_offset(over_x, 1, 0)
    opposite = from_offset(over_x, 2, 0)
    acc = add(acc, peak, [over_x, over_y], 5, 2)
    acc, diag_left, diag_right = lax.optimization_barrier((acc, diag_left, diag_right))
    acc = add(acc, peak, [diag_left, diag_right], 7, 4)
    last = [far_left, far_right, far_up, far_down, opposite]
    acc, *last = lax.optimization_barrier((acc, *last))
    everything = [own, left, right, up, down, over_x, over_y, diag_left, diag_right] + last
    return end(acc, peak, last, 11, 5, everything)


def solution(mesh):
    both = P(("batch", "ctx"), "head")
    placed = (both, both, both, both, both, P("batch"), P("batch"))
    return jax.shard_map(shards, mesh=mesh, in_specs=placed, out_specs=both, check_vma=False)
```

profile of v0, /device:TPU:62, one launch (start us, length us, event | category | flops | bytes accessed | tf_op | source)
XLA Modules:
  0.0 157.7 jit_solution(1904243655128992436)
XLA Ops:
  0.0 0.9 constant_dynamic-update-slice_fusion.3
  0.9 0.8 constant_dynamic-update-slice_fusion.2
  1.7 0.9 constant_dynamic-update-slice_fusion.1
  2.6 0.8 constant_dynamic-update-slice_fusion.kv_ref.refs_5_
  3.4 0.2 collective-permute-start
  3.6 1.8 %collective-permute-start.1 = (bf16[1280,128]{1,0:T(8,128)(2,1)S(1)}, bf16[1280,128]{1,0:T(8,128)(2,1)S(1)}, u32[]{:S(2)}, u32[]{:S(2)}) collective-permute-start(bf16[1280,128]{1,0:T(8,128)(2,1)S(1)} %constant_dynamic-update-slice_fusion.kv_ref.refs_5_), channel_id=1, source_target_pairs={{64,0},{80,16},{96,32},{112,48},{128,64},{144,80},{160,96},{176,11... | collective-permute-start | bytes 983048 | tf_op jit(solution)/shard_map/ppermute | solution.py:30
  5.4 0.5 collective-permute-start.2
  5.9 1.5 collective-permute-start.3
  7.4 0.7 fusion.src_ref
  8.1 1.0 copy-done
  9.2 0.7 copy-done.1
  9.9 0.7 copy-done.2
  10.5 4.4 %shard_map.82 = (f32[2048,256]{1,0:T(8,128)S(1)}, f32[4,128,128]{2,1,0:T(8,128)S(1)}) custom-call(s32[16]{0:T(128)S(1)} %fusion.src_ref, s32[16]{0:T(128)S(1)} %copy-done.2, bf16[128,2048]{1,0:T(8,128)(2,1)S(1)} %copy-done, s32[16,128]{1,0:T(8,128)S(1)} %bitcast.5, bf16[1280,128]{1,0:T(8,128)(2,1)S(1)} %constant_dynamic-update-slice_fusion.kv_ref.refs_5_), custom_call_target="tpu_custom_call" | custom-call | tf_op jit(solution)/shard_map/pallas_call | solution.py:196
  15.0 0.0 collective-permute-done.1.refs_3_.refs_9_
  15.0 0.0 collective-permute-done.2.refs_0_.refs_6_
  15.0 0.7 collective-permute-done.3.refs_1_.refs_7_
  15.8 1.1 collective-permute-start.6
  16.9 1.0 collective-permute-start.7
  17.9 1.2 collective-permute-start.4
  19.1 1.2 collective-permute-start.5
  20.3 9.1 %shard_map.83.acc_in = f32[2048,256]{1,0:T(8,128)S(1)} custom-call(s32[16]{0:T(128)S(1)} %fusion.src_ref, s32[16]{0:T(128)S(1)} %copy-done.2, bf16[128,2048]{1,0:T(8,128)(2,1)S(1)} %copy-done, s32[16,128]{1,0:T(8,128)S(1)} %bitcast.6, f32[4,128,128]{2,1,0:T(8,128)S(1)} %get-tuple-element.24.m_ref, ...), custom_call_target="tpu_custom_call", output_to_operand_aliasing={{}: (5, {})} | custom-call | tf_op jit(solution)/shard_map/pallas_call | solution.py:207
  29.5 0.0 collective-permute-done.4.refs_1_.refs_11_
  29.5 9.4 %collective-permute-done.5.refs_0_.refs_10_ = bf16[1280,128]{1,0:T(8,128)(2,1)S(1)} collective-permute-done((bf16[1280,128]{1,0:T(8,128)(2,1)S(1)}, bf16[1280,128]{1,0:T(8,128)(2,1)S(1)}, u32[]{:S(2)}, u32[]{:S(2)}) %collective-permute-start.5) | collective-permute-done | bytes 327712 | tf_op jit(solution)/shard_map/ppermute | solution.py:30
  38.9 1.6 collective-permute-start.10
  40.4 0.5 collective-permute-start.11
  40.9 1.2 collective-permute-start.12
  42.1 1.5 collective-permute-start.8
  43.6 0.5 collective-permute-start.9
  44.2 5.3 %shard_map.84.acc_in = f32[2048,256]{1,0:T(8,128)S(1)} custom-call(s32[16]{0:T(128)S(1)} %fusion.src_ref, s32[16]{0:T(128)S(1)} %copy-done.2, bf16[128,2048]{1,0:T(8,128)(2,1)S(1)} %copy-done, s32[16,128]{1,0:T(8,128)S(1)} %bitcast.7, f32[4,128,128]{2,1,0:T(8,128)S(1)} %get-tuple-element.24.m_ref, ...), custom_call_target="tpu_custom_call", output_to_operand_aliasing={{}: (5, {})} | custom-call | tf_op jit(solution)/shard_map/pallas_call | solution.py:207
  49.5 9.2 %shard_map.85.acc_in = f32[2048,256]{1,0:T(8,128)S(1)} custom-call(s32[16]{0:T(128)S(1)} %fusion.src_ref, s32[16]{0:T(128)S(1)} %copy-done.2, bf16[128,2048]{1,0:T(8,128)(2,1)S(1)} %copy-done, s32[16,128]{1,0:T(8,128)S(1)} %bitcast.8, f32[4,128,128]{2,1,0:T(8,128)S(1)} %get-tuple-element.24.m_ref, ...), custom_call_target="tpu_custom_call", output_to_operand_aliasing={{}: (5, {})} | custom-call | tf_op jit(solution)/shard_map/pallas_call | solution.py:207
  58.7 0.0 collective-permute-done.11.refs_3_.refs_17_
  58.7 98.8 %shard_map.86 = bf16[128,2048]{1,0:T(8,128)(2,1)} custom-call(s32[16]{0:T(128)S(1)} %fusion.src_ref, s32[16]{0:T(128)S(1)} %copy-done.2, bf16[128,2048]{1,0:T(8,128)(2,1)S(1)} %copy-done, s32[16,128]{1,0:T(8,128)S(1)} %bitcast.9, f32[4,128,128]{2,1,0:T(8,128)S(1)} %get-tuple-element.24.m_ref, f32[2048,256]{1,0:T(8,128)S(1)} %shard_map.85.acc_in, ...), custom_call_target="tpu_custom_call" | custom-call | tf_op jit(solution)/shard_map/pallas_call | solution.py:219
  (12 shorter events, 0.1 us)
Async XLA Ops:
  3.4 11.6 %collective-permute-start = (bf16[1280,128]{1,0:T(8,128)(2,1)S(1)}, bf16[1280,128]{1,0:T(8,128)(2,1)S(1)}, u32[]{:S(2)}, u32[]{:S(2)}) collective-permute-start(bf16[1280,128]{1,0:T(8,128)(2,1)S(1)} %constant_dynamic-update-slice_fusion.kv_ref.refs_5_), channel_id=1, source_target_pairs={{192,0},{208,16},{224,32},{240,48},{0,64},{16,80},{32,96},{48,112}... | collective-permute-start | bytes 983048 | tf_op jit(solution)/shard_map/ppermute | solution.py:30
  3.6 11.4 %collective-permute-start.1 = (bf16[1280,128]{1,0:T(8,128)(2,1)S(1)}, bf16[1280,128]{1,0:T(8,128)(2,1)S(1)}, u32[]{:S(2)}, u32[]{:S(2)}) collective-permute-start(bf16[1280,128]{1,0:T(8,128)(2,1)S(1)} %constant_dynamic-update-slice_fusion.kv_ref.refs_5_), channel_id=1, source_target_pairs={{64,0},{80,16},{96,32},{112,48},{128,64},{144,80},{160,96},{176,11... | collective-permute-start | bytes 983048 | tf_op jit(solution)/shard_map/ppermute | solution.py:30
  5.4 9.6 %collective-permute-start.2 = (bf16[1280,128]{1,0:T(8,128)(2,1)S(1)}, bf16[1280,128]{1,0:T(8,128)(2,1)S(1)}, u32[]{:S(2)}, u32[]{:S(2)}) collective-permute-start(bf16[1280,128]{1,0:T(8,128)(2,1)S(1)} %constant_dynamic-update-slice_fusion.kv_ref.refs_5_), channel_id=1, source_target_pairs={{48,0},{0,16},{16,32},{32,48},{112,64},{64,80},{80,96},{96,112},{1... | collective-permute-start | bytes 983048 | tf_op jit(solution)/shard_map/ppermute | solution.py:30
  5.9 9.8 %collective-permute-start.3 = (bf16[1280,128]{1,0:T(8,128)(2,1)S(1)}, bf16[1280,128]{1,0:T(8,128)(2,1)S(1)}, u32[]{:S(2)}, u32[]{:S(2)}) collective-permute-start(bf16[1280,128]{1,0:T(8,128)(2,1)S(1)} %constant_dynamic-update-slice_fusion.kv_ref.refs_5_), channel_id=1, source_target_pairs={{16,0},{32,16},{48,32},{0,48},{80,64},{96,80},{112,96},{64,112},{1... | collective-permute-start | bytes 983048 | tf_op jit(solution)/shard_map/ppermute | solution.py:30
  8.1 1.0 copy-start
  9.2 0.7 copy-start.1
  9.9 0.7 copy-start.2
  15.8 26.3 %collective-permute-start.6 = (bf16[2560,128]{1,0:T(8,128)(2,1)S(1)}, bf16[2560,128]{1,0:T(8,128)(2,1)S(1)}, u32[]{:S(2)}, u32[]{:S(2)}) collective-permute-start(bf16[2560,128]{1,0:T(8,128)(2,1)S(1)} %constant_dynamic-update-slice_fusion.4), channel_id=1, source_target_pairs={{48,0},{0,16},{16,32},{32,48},{112,64},{64,80},{80,96},{96,112},{1... | collective-permute-start | bytes 1966088 | tf_op jit(solution)/shard_map/ppermute | solution.py:30
  16.9 26.8 %collective-permute-start.7 = (bf16[2560,128]{1,0:T(8,128)(2,1)S(1)}, bf16[2560,128]{1,0:T(8,128)(2,1)S(1)}, u32[]{:S(2)}, u32[]{:S(2)}) collective-permute-start(bf16[2560,128]{1,0:T(8,128)(2,1)S(1)} %constant_dynamic-update-slice_fusion.4), channel_id=1, source_target_pairs={{16,0},{32,16},{48,32},{0,48},{80,64},{96,80},{112,96},{64,112},{1... | collective-permute-start | bytes 1966088 | tf_op jit(solution)/shard_map/ppermute | solution.py:30
  17.9 11.6 %collective-permute-start.4 = (bf16[1280,128]{1,0:T(8,128)(2,1)S(1)}, bf16[1280,128]{1,0:T(8,128)(2,1)S(1)}, u32[]{:S(2)}, u32[]{:S(2)}) collective-permute-start(bf16[1280,128]{1,0:T(8,128)(2,1)S(1)} %constant_dynamic-update-slice_fusion.kv_ref.refs_5_), channel_id=1, source_target_pairs={{128,0},{144,16},{160,32},{176,48},{192,64},{208,80},{224,96},{240... | collective-permute-start | bytes 983048 | tf_op jit(solution)/shard_map/ppermute | solution.py:30
  19.1 19.7 %collective-permute-start.5 = (bf16[1280,128]{1,0:T(8,128)(2,1)S(1)}, bf16[1280,128]{1,0:T(8,128)(2,1)S(1)}, u32[]{:S(2)}, u32[]{:S(2)}) collective-permute-start(bf16[1280,128]{1,0:T(8,128)(2,1)S(1)} %constant_dynamic-update-slice_fusion.kv_ref.refs_5_), channel_id=1, source_target_pairs={{32,0},{48,16},{0,32},{16,48},{96,64},{112,80},{64,96},{80,112},{1... | collective-permute-start | bytes 983048 | tf_op jit(solution)/shard_map/ppermute | solution.py:30
  38.9 19.8 %collective-permute-start.10 = (bf16[1280,128]{1,0:T(8,128)(2,1)S(1)}, bf16[1280,128]{1,0:T(8,128)(2,1)S(1)}, u32[]{:S(2)}, u32[]{:S(2)}) collective-permute-start(bf16[1280,128]{1,0:T(8,128)(2,1)S(1)} %collective-permute-done.5.refs_0_.refs_10_), channel_id=1, source_target_pairs={{192,0},{208,16},{224,32},{240,48},{0,64},{16,80},{32,96},{48,112}... | collective-permute-start | bytes 983048 | tf_op jit(solution)/shard_map/ppermute | solution.py:30
  40.4 18.3 %collective-permute-start.11 = (bf16[1280,128]{1,0:T(8,128)(2,1)S(1)}, bf16[1280,128]{1,0:T(8,128)(2,1)S(1)}, u32[]{:S(2)}, u32[]{:S(2)}) collective-permute-start(bf16[1280,128]{1,0:T(8,128)(2,1)S(1)} %collective-permute-done.5.refs_0_.refs_10_), channel_id=1, source_target_pairs={{64,0},{80,16},{96,32},{112,48},{128,64},{144,80},{160,96},{176,11... | collective-permute-start | bytes 983048 | tf_op jit(solution)/shard_map/ppermute | solution.py:30
  40.9 17.8 %collective-permute-start.12 = (bf16[1280,128]{1,0:T(8,128)(2,1)S(1)}, bf16[1280,128]{1,0:T(8,128)(2,1)S(1)}, u32[]{:S(2)}, u32[]{:S(2)}) collective-permute-start(bf16[1280,128]{1,0:T(8,128)(2,1)S(1)} %collective-permute-done.5.refs_0_.refs_10_), channel_id=1, source_target_pairs={{128,0},{144,16},{160,32},{176,48},{192,64},{208,80},{224,96},{240... | collective-permute-start | bytes 983048 | tf_op jit(solution)/shard_map/ppermute | solution.py:30
  42.1 16.6 %collective-permute-start.8 = (bf16[1280,128]{1,0:T(8,128)(2,1)S(1)}, bf16[1280,128]{1,0:T(8,128)(2,1)S(1)}, u32[]{:S(2)}, u32[]{:S(2)}) collective-permute-start(bf16[1280,128]{1,0:T(8,128)(2,1)S(1)} %collective-permute-done.4.refs_1_.refs_11_), channel_id=1, source_target_pairs={{48,0},{0,16},{16,32},{32,48},{112,64},{64,80},{80,96},{96,112},{1... | collective-permute-start | bytes 983048 | tf_op jit(solution)/shard_map/ppermute | solution.py:30
  43.6 15.1 %collective-permute-start.9 = (bf16[1280,128]{1,0:T(8,128)(2,1)S(1)}, bf16[1280,128]{1,0:T(8,128)(2,1)S(1)}, u32[]{:S(2)}, u32[]{:S(2)}) collective-permute-start(bf16[1280,128]{1,0:T(8,128)(2,1)S(1)} %collective-permute-done.4.refs_1_.refs_11_), channel_id=1, source_target_pairs={{16,0},{32,16},{48,32},{0,48},{80,64},{96,80},{112,96},{64,112},{1... | collective-permute-start | bytes 983048 | tf_op jit(solution)/shard_map/ppermute | solution.py:30
where the time goes:
time: 158 us
  Pallas kernels  127 us (80%)
  starting transfers between devices  13.9 us (9%)
  waiting for transfers between devices  10.1 us (6%)
  local copies, waits for them, and re-layouts  5.83 us (4%)
    pallas_call x1, Pallas kernels, end(): pl.pallas_call(functools.partial(last_kernel, first=first, count=count, p...  98.8 us
    pallas_call x3, Pallas kernels, add(): pl.pallas_call(functools.partial(middle_kernel, first=first, count=count,...  23.6 us
    ppermute x13, starting transfers between devices, from_offset(): return lax.ppermute(block, 'ctx', route)  13.9 us
    ppermute x13, waiting for transfers between devices, from_offset(): return lax.ppermute(block, 'ctx', route)  10.1 us
    unnamed x10, local copies, waits for them, and re-layouts  5.02 us
    pallas_call x1, Pallas kernels, begin(): pl.pallas_call(functools.partial(first_kernel, cached=cached, tokens=toke...  4.44 us
  transfers between devices with their start and end apart: 13, of which 2 were waited for; matrix products, arithmetic and copies ran while one was open for 0% of the time, Pallas kernels for 18%

commit v1 on v0

v1 whole, which is shorter than its diff:
```python
import functools
import jax
import jax.numpy as jnp
from jax import lax
from jax.experimental import pallas as pl
from jax.experimental.pallas import tpu as pltpu
from jax.sharding import PartitionSpec as P

HD = 128
SIDE = 4
HG = 8
NEG = -1e30
LIMIT = 1e37
VMEM = 40 * 2**20
LOG2E = 1.4426950408889634

ORDER = (
    (0, 0),
    (-1, 0), (1, 0), (0, -1), (0, 1), (0, 2),
    (2, 0), (-1, -1), (1, -1), (-1, 1), (1, 1),
    (-1, 2), (1, 2), (2, 2), (2, -1), (2, 1),
)


def from_offset(block, dy, dx):
    route = []
    for y in range(SIDE):
        for x in range(SIDE):
            route.append((((y + dy) % SIDE) * SIDE + (x + dx) % SIDE, y * SIDE + x))
    return lax.ppermute(block, "ctx", route)


def rows_of(q_ref):
    return jnp.concatenate([q_ref[:, i * HD:(i + 1) * HD] for i in range(HG)], 0)


def source(slot):
    here = lax.axis_index("ctx")
    dy, dx = ORDER[slot]
    return ((here // SIDE + dy + SIDE) % SIDE) * SIDE + (here % SIDE + dx + SIDE) % SIDE


def pack_kernel(lens_ref, ck_ref, nk_ref, cv_ref, nv_ref, q_ref, pos_ref, out_ref, q_out, meta_ref,
                keys_ref, values_ref, posbuf_ref, lensbuf_ref, sems):
    cached, tokens = ck_ref.shape[0], nk_ref.shape[0]
    width = cached + tokens
    moves = [
        (ck_ref, keys_ref.at[pl.ds(0, cached)]),
        (nk_ref, keys_ref.at[pl.ds(cached, tokens)]),
        (cv_ref, values_ref),
        (nv_ref, out_ref.at[pl.ds(width + cached, tokens)]),
        (pos_ref, posbuf_ref),
        (q_ref, q_out),
        (lens_ref, lensbuf_ref),
    ]
    copies = [pltpu.make_async_copy(src, dst, sems.at[i]) for i, (src, dst) in enumerate(moves)]
    for copy in copies:
        copy.start()
    copies[6].wait()
    for slot in range(len(ORDER)):
        meta_ref[len(ORDER) + slot:len(ORDER) + slot + 1, :] = jnp.full((1, HD), lensbuf_ref[source(slot)], jnp.int32)
    copies[0].wait()
    copies[1].wait()
    for t in range(width // HD):
        out_ref[t * HD:(t + 1) * HD, :] = keys_ref[t * HD:(t + 1) * HD, :].T
    copies[2].wait()
    valid = lax.broadcasted_iota(jnp.int32, (cached, HD), 0) < meta_ref[len(ORDER):len(ORDER) + 1, :]
    stored = values_ref[...]
    out_ref[width:width + cached, :] = jnp.where(valid, stored, jnp.zeros_like(stored))
    copies[4].wait()
    for slot in range(len(ORDER)):
        meta_ref[slot:slot + 1, :] = posbuf_ref[pl.ds(source(slot), 1), :]
    copies[3].wait()
    copies[5].wait()


def blocks_of(refs, width):
    return [(ref, part * 2 * width) for ref in refs for part in range(ref.shape[0] // (2 * width))]


def keys_at(tiles):
    return jnp.concatenate([ref[base + t * HD:base + (t + 1) * HD, :] for ref, base, _, t in tiles], 1)


def values_at(tiles, ones_ref, cached, tokens):
    values, ones = [], []
    for ref, base, b, t in tiles:
        at = base + cached + tokens + t * HD
        values.append(ref[at:at + HD, :])
        ones.append(ones_ref[b, t * HD:(t + 1) * HD, :] if t < cached // HD else jnp.ones((HD, HD), jnp.bfloat16))
    return jnp.concatenate([jnp.concatenate(values, 0), jnp.concatenate(ones, 0)], 1)


def fill_ones(meta_ref, ones_ref, first, count, cached):
    for b in range(count):
        row = len(ORDER) + first + b
        valid = lax.broadcasted_iota(jnp.int32, (cached, HD), 0) < meta_ref[row:row + 1, :]
        ones_ref[b] = jnp.where(valid, 1.0, 0.0).astype(jnp.bfloat16)


def first_kernel(q_ref, meta_ref, kv_ref, acc_ref, m_ref, mask_ref, ones_ref, *, cached, tokens):
    width = cached + tokens

    @pl.when(pl.program_id(0) == 0)
    def _():
        fill_ones(meta_ref, ones_ref, 0, 1, cached)
        own = jnp.broadcast_to(meta_ref[0:1, :], (tokens, tokens)).T
        for slot in range(len(ORDER)):
            seen = meta_ref[slot:slot + 1, :] <= own
            mask_ref[slot] = jnp.where(seen, 1.0, 0.0).astype(jnp.bfloat16)

    scale = LOG2E * HD ** -0.5
    q = rows_of(q_ref)
    tiles = [(kv_ref, 0, 0, t) for t in range(width // HD)]
    scores = jnp.dot(q, keys_at(tiles), preferred_element_type=jnp.float32) * scale
    lane = lax.broadcasted_iota(jnp.int32, (1, cached), 1)
    length = jnp.concatenate([meta_ref[len(ORDER):len(ORDER) + 1, :]] * (cached // HD), 1)
    bias = jnp.where(lane < length, 0.0, NEG)
    shown = jnp.concatenate([mask_ref[0].astype(jnp.float32)] * HG, 0) > 0.5
    scores = jnp.concatenate([scores[:, :cached] + bias, jnp.where(shown, scores[:, cached:], NEG)], 1)
    peak = jnp.max(scores, 1, keepdims=True)
    weights = jnp.exp2(scores - peak).astype(jnp.bfloat16)
    values = values_at(tiles, ones_ref, cached, tokens)
    acc_ref[...] = jnp.dot(weights, values, preferred_element_type=jnp.float32)
    for i in range(HG):
        m_ref[0, :, i:i + 1] = peak[i * tokens:(i + 1) * tokens, :]


def add_blocks(q_ref, m_ref, mask_ref, acc, kv_refs, ones_ref, first, cached, tokens):
    width = cached + tokens
    scale = LOG2E * HD ** -0.5
    full = cached // HD
    q = rows_of(q_ref)
    peak = jnp.concatenate([m_ref[0, :, i:i + 1] for i in range(HG)], 0)
    blocks = [(ref, base, b) for b, (ref, base) in enumerate(blocks_of(kv_refs, width))]
    for p in range(0, len(blocks), 2):
        pair = blocks[p:p + 2]
        tiles = [block + (t,) for block in pair for t in range(full)]
        tiles += [block + (t,) for block in pair for t in range(full, width // HD)]
        scores = jnp.dot(q, keys_at(tiles), preferred_element_type=jnp.float32)
        weights = jnp.exp2(scores * scale - peak).astype(jnp.bfloat16)
        at = len(pair) * cached
        parts = [weights[:, :at]]
        for i, (_, _, b) in enumerate(pair):
            seen = jnp.concatenate([mask_ref[first + b]] * HG, 0)
            parts.append(weights[:, at + i * tokens:at + (i + 1) * tokens] * seen)
        values = values_at(tiles, ones_ref, cached, tokens)
        acc = acc + jnp.dot(jnp.concatenate(parts, 1), values, preferred_element_type=jnp.float32)
    return acc


def middle_kernel(meta_ref, q_ref, m_ref, mask_ref, acc_in, *refs, first, count, cached, tokens):
    kv_refs, (acc_out, ones_ref) = refs[:-2], refs[-2:]

    @pl.when(pl.program_id(0) == 0)
    def _():
        fill_ones(meta_ref, ones_ref, first, count, cached)

    acc_out[...] = add_blocks(q_ref, m_ref, mask_ref, acc_in[...], kv_refs, ones_ref, first, cached, tokens)


def safe_rows(q_ref, mask_ref, acc_ref, peak_ref, everything, all_ref, sem, meta_ref, cached, tokens):
    width = cached + tokens
    scale = LOG2E * HD ** -0.5
    for slot, (ref, base) in enumerate(blocks_of(everything, width)):
        copy = pltpu.make_async_copy(ref.at[pl.ds(base, 2 * width)], all_ref.at[slot], sem)
        copy.start()
        copy.wait()
    q = rows_of(q_ref)
    peak_ref[...] = jnp.full(peak_ref.shape, NEG, jnp.float32)
    acc_ref[...] = jnp.zeros(acc_ref.shape, jnp.float32)

    def step(b, carry):
        keys = jnp.concatenate([all_ref[b, t * HD:(t + 1) * HD, :] for t in range(width // HD)], 1)
        scores = jnp.dot(q, keys, preferred_element_type=jnp.float32) * scale
        lane = lax.broadcasted_iota(jnp.int32, (tokens, cached), 1)
        length = jnp.concatenate([meta_ref[pl.ds(len(ORDER) + b, 1), :]] * (cached // HD), 1)
        filled = jnp.where(lane < length, 1.0, 0.0)
        seen = mask_ref[b].astype(jnp.float32)
        shown = jnp.concatenate([jnp.concatenate([filled, seen], 1)] * HG, 0) > 0.5
        scores = jnp.where(shown, scores, NEG)
        old = peak_ref[...]
        new = jnp.maximum(old, jnp.max(scores, 1, keepdims=True))
        weights = jnp.where(shown, jnp.exp2(scores - new[:, :1]), 0.0).astype(jnp.bfloat16)
        values = jnp.concatenate([all_ref[b, width:, :], jnp.ones((width, HD), jnp.bfloat16)], 1)
        factor = jnp.exp2(old - new)
        acc_ref[...] = acc_ref[...] * factor[:, :1] + jnp.dot(weights, values, preferred_element_type=jnp.float32)
        peak_ref[...] = new
        return carry

    lax.fori_loop(0, len(ORDER), step, 0)


def last_kernel(meta_ref, q_ref, m_ref, mask_ref, acc_in, *refs, first, count, parts, others, cached, tokens):
    kv_refs, others_refs = refs[:parts], refs[parts:parts + others]
    out_ref, ones_ref, acc_ref, peak_ref, all_ref, sem = refs[parts + others:]

    @pl.when(pl.program_id(0) == 0)
    def _():
        fill_ones(meta_ref, ones_ref, first, count, cached)

    def finish(acc):
        result = (acc[:, :HD] / acc[:, HD:]).astype(jnp.bfloat16)
        for i in range(HG):
            out_ref[:, i * HD:(i + 1) * HD] = result[i * tokens:(i + 1) * tokens, :]

    acc = add_blocks(q_ref, m_ref, mask_ref, acc_in[...], kv_refs, ones_ref, first, cached, tokens)
    finish(acc)
    bad = jnp.max(jnp.where(acc[:, HD:] < LIMIT, 0.0, 1.0)) > 0.5

    @pl.when(bad)
    def _():
        safe_rows(q_ref, mask_ref, acc_ref, peak_ref, others_refs, all_ref, sem, meta_ref, cached, tokens)
        finish(acc_ref[...])


def shards(queries, new_keys, new_values, cache_keys, cache_values, cache_lens, new_pos):
    tokens, cached = new_keys.shape[0], cache_keys.shape[0]
    width = cached + tokens
    groups = queries.shape[1] // (HG * HD)
    rows = HG * tokens
    positions = new_pos.reshape(-1, tokens)

    whole = pl.BlockSpec(memory_space=pltpu.VMEM)
    head_block = pl.BlockSpec((tokens, HG * HD), lambda g: (0, g))
    acc_block = pl.BlockSpec((rows, 2 * HD), lambda g: (g, 0))
    peak_block = pl.BlockSpec((1, tokens, HD), lambda g: (g, 0, 0))
    acc_shape = jax.ShapeDtypeStruct((groups * rows, 2 * HD), jnp.float32)
    peak_shape = jax.ShapeDtypeStruct((groups, tokens, HD), jnp.float32)
    mask_shape = jax.ShapeDtypeStruct((len(ORDER), tokens, tokens), jnp.bfloat16)
    params = pltpu.CompilerParams(vmem_limit_bytes=VMEM)
    cost = pl.CostEstimate(flops=1, bytes_accessed=1, transcendentals=0)

    def ones(blocks):
        return pltpu.VMEM((blocks, cached, HD), jnp.bfloat16)

    def pack():
        return pl.pallas_call(
            pack_kernel,
            in_specs=[pl.BlockSpec(memory_space=pltpu.HBM)] * 7,
            out_specs=[whole] * 3,
            out_shape=[
                pltpu.VMEM((2 * width, HD), jnp.bfloat16),
                pltpu.VMEM(queries.shape, jnp.bfloat16),
                pltpu.VMEM((2 * len(ORDER), tokens), jnp.int32),
            ],
            scratch_shapes=[
                pltpu.VMEM((width, HD), jnp.bfloat16),
                pltpu.VMEM((cached, HD), jnp.bfloat16),
                pltpu.VMEM(positions.shape, jnp.int32),
                pltpu.SMEM(cache_lens.shape, jnp.int32),
                pltpu.SemaphoreType.DMA((7,)),
            ],
            compiler_params=params,
            cost_estimate=cost,
        )(*[
            pltpu.with_memory_space_constraint(part, pltpu.HBM)
            for part in (cache_lens, cache_keys, new_keys, cache_values, new_values, queries, positions)
        ])

    def begin(own):
        return pl.pallas_call(
            functools.partial(first_kernel, cached=cached, tokens=tokens),
            grid=(groups,),
            in_specs=[head_block, whole, whole],
            out_specs=[acc_block, peak_block, whole],
            out_shape=[acc_shape, peak_shape, mask_shape],
            scratch_shapes=[ones(1)],
            compiler_params=params,
            cost_estimate=cost,
        )(query, meta, own)

    def add(acc, peak, mask, parts, first, count):
        return pl.pallas_call(
            functools.partial(middle_kernel, first=first, count=count, cached=cached, tokens=tokens),
            grid=(groups,),
            in_specs=[whole, head_block, peak_block, whole, acc_block] + [whole] * len(parts),
            out_specs=acc_block,
            out_shape=acc_shape,
            input_output_aliases={4: 0},
            scratch_shapes=[ones(count)],
            compiler_params=params,
            cost_estimate=cost,
        )(meta, query, peak, mask, acc, *parts)

    def end(acc, peak, mask, parts, first, count, everything):
        return pl.pallas_call(
            functools.partial(last_kernel, first=first, count=count, parts=len(parts), others=len(everything),
                              cached=cached, tokens=tokens),
            grid=(groups,),
            in_specs=[whole, head_block, peak_block, whole, acc_block] + [whole] * (len(parts) + len(everything)),
            out_specs=head_block,
            out_shape=jax.ShapeDtypeStruct(queries.shape, jnp.bfloat16),
            scratch_shapes=[
                ones(count),
                pltpu.VMEM((rows, 2 * HD), jnp.float32),
                pltpu.VMEM((rows, HD), jnp.float32),
                pltpu.VMEM((len(ORDER), 2 * width, HD), jnp.bfloat16),
                pltpu.SemaphoreType.DMA,
            ],
            compiler_params=params,
            cost_estimate=cost,
        )(meta, query, peak, mask, acc, *parts, *everything)

    tie = lax.optimization_barrier
    own, query, meta = pack()
    up, down = from_offset(own, -1, 0), from_offset(own, 1, 0)
    left, right = from_offset(own, 0, -1), from_offset(own, 0, 1)
    over_x = from_offset(own, 0, 2)
    acc, peak, mask = begin(own)

    acc, up, down = tie((acc, up, down))
    acc = add(acc, peak, mask, [up, down], 1, 2)

    acc, own_later, up, down, left, right, over_x = tie((acc, own, up, down, left, right, over_x))
    column = jnp.concatenate([up, down], 0)
    diag_left, diag_right = from_offset(column, 0, -1), from_offset(column, 0, 1)
    over_y = from_offset(own_later, 2, 0)
    far_up, far_down = from_offset(over_x, -1, 0), from_offset(over_x, 1, 0)
    acc = add(acc, peak, mask, [left, right, over_x], 3, 3)

    acc, over_y, over_x_later = tie((acc, over_y, over_x))
    far_left, far_right = from_offset(over_y, 0, -1), from_offset(over_y, 0, 1)
    opposite = from_offset(over_x_later, 2, 0)
    acc, diag_left, diag_right, over_y_later = tie((acc, diag_left, diag_right, over_y))
    acc = add(acc, peak, mask, [over_y_later, diag_left, diag_right], 6, 5)

    last = [far_up, far_down, opposite, far_left, far_right]
    acc, *last = tie((acc, *last))
    everything = [own, up, down, left, right, over_x, over_y, diag_left, diag_right]
    return end(acc, peak, mask, last, 11, 5, everything + last)


def solution(mesh):
    both = P(("batch", "ctx"), "head")
    placed = (both, both, both, both, both, P("batch"), P("batch"))
    return jax.shard_map(shards, mesh=mesh, in_specs=placed, out_specs=both, check_vma=False)
```

time: 158 us -> 118 us (0.75)
  Pallas kernels: 127 us -> 92.5 us
  local copies, waits for them, and re-layouts: 5.83 us -> 0.07 us
    pallas_call x1, Pallas kernels: 98.8 us -> 71.1 us  [end(): pl.pallas_call(functools.partial(last_kernel, first=first, count=count, p...]
    pallas_call x3, Pallas kernels: 23.6 us -> 17 us  [add(): pl.pallas_call(functools.partial(middle_kernel, first=first, count=count,...]
    unnamed x10 -> x1, local copies, waits for them, and re-layouts: 5.02 us -> 0.02 us
  transfers between devices with their start and end apart: 13 -> 13, of which waited for: 2 -> 5; matrix products, arithmetic and copies ran while one was open for 0% -> 0% of each run, Pallas kernels for 18% -> 17%
where the time goes in v1:
time: 118 us
  Pallas kernels  92.5 us (78%)
  starting transfers between devices  14.7 us (12%)
  waiting for transfers between devices  10.8 us (9%)
    pallas_call x1, Pallas kernels, end(): pl.pallas_call(functools.partial(last_kernel, first=first, count=count, p...  71.1 us
    pallas_call x3, Pallas kernels, add(): pl.pallas_call(functools.partial(middle_kernel, first=first, count=count,...  17 us
    ppermute x13, starting transfers between devices, from_offset(): return lax.ppermute(block, 'ctx', route)  14.7 us
    ppermute x13, waiting for transfers between devices, from_offset(): return lax.ppermute(block, 'ctx', route)  10.8 us
    pallas_call x1, Pallas kernels, begin(): pl.pallas_call(functools.partial(first_kernel, cached=cached, tokens=toke...  3.1 us
  transfers between devices with their start and end apart: 13, of which 5 were waited for; matrix products, arithmetic and copies ran while one was open for 0% of the time, Pallas kernels for 17%

profile of v1, /device:TPU:62, one launch (start us, length us, event | category | flops | bytes accessed | tf_op | source)
XLA Modules:
  0.0 118.4 jit_solution(1780316510280395290)
XLA Ops:
  0.0 1.3 %shard_map.73 = (bf16[1280,128]{1,0:T(8,128)(2,1)S(1)}, bf16[128,2048]{1,0:T(8,128)(2,1)S(1)}, s32[32,128]{1,0:T(8,128)S(1)}) custom-call(s32[16]{0:T(128)} %lens_ref.1, bf16[512,128]{1,0:T(8,128)(2,1)} %ck_ref.1, bf16[128,128]{1,0:T(8,128)(2,1)} %nk_ref.1, bf16[512,128]{1,0:T(8,128)(2,1)} %cv_ref.1, bf16[128,128]{1,0:T(8,128)(2,1)} %nv_ref.1, ...), custom_call_target="tpu_custom_call" | custom-call | flops 1 | bytes 1 | tf_op jit(solution)/shard_map/pallas_call | solution.py:238
  1.3 0.3 collective-permute-start
  1.6 1.8 %collective-permute-start.1 = (bf16[1280,128]{1,0:T(8,128)(2,1)S(1)}, bf16[1280,128]{1,0:T(8,128)(2,1)S(1)}, u32[]{:S(2)}, u32[]{:S(2)}) collective-permute-start(bf16[1280,128]{1,0:T(8,128)(2,1)S(1)} %get-tuple-element.47.kv_ref.refs_5_), channel_id=1, source_target_pairs={{64,0},{80,16},{96,32},{112,48},{128,64},{144,80},{160,96},{176,11... | collective-permute-start | bytes 983048 | tf_op jit(solution)/shard_map/ppermute | solution.py:30
  3.4 0.5 collective-permute-start.2
  3.9 1.5 %collective-permute-start.3 = (bf16[1280,128]{1,0:T(8,128)(2,1)S(1)}, bf16[1280,128]{1,0:T(8,128)(2,1)S(1)}, u32[]{:S(2)}, u32[]{:S(2)}) collective-permute-start(bf16[1280,128]{1,0:T(8,128)(2,1)S(1)} %get-tuple-element.47.kv_ref.refs_5_), channel_id=1, source_target_pairs={{16,0},{32,16},{48,32},{0,48},{80,64},{96,80},{112,96},{64,112},{1... | collective-permute-start | bytes 983048 | tf_op jit(solution)/shard_map/ppermute | solution.py:30
  5.4 1.4 %collective-permute-start.4 = (bf16[1280,128]{1,0:T(8,128)(2,1)S(1)}, bf16[1280,128]{1,0:T(8,128)(2,1)S(1)}, u32[]{:S(2)}, u32[]{:S(2)}) collective-permute-start(bf16[1280,128]{1,0:T(8,128)(2,1)S(1)} %get-tuple-element.47.kv_ref.refs_5_), channel_id=1, source_target_pairs={{32,0},{48,16},{0,32},{16,48},{96,64},{112,80},{64,96},{80,112},{1... | collective-permute-start | bytes 983048 | tf_op jit(solution)/shard_map/ppermute | solution.py:30
  6.8 3.1 %shard_map.74 = (f32[2048,256]{1,0:T(8,128)S(1)}, f32[2,128,128]{2,1,0:T(8,128)S(1)}, bf16[16,128,128]{2,1,0:T(8,128)(2,1)S(1)}) custom-call(bf16[128,2048]{1,0:T(8,128)(2,1)S(1)} %get-tuple-element.35.q_ref, s32[32,128]{1,0:T(8,128)S(1)} %get-tuple-element.34.meta_ref, bf16[1280,128]{1,0:T(8,128)(2,1)S(1)} %get-tuple-element.47.kv_ref.refs_5_), custom_call_target="tpu_custom_call" | custom-call | flops 1 | bytes 1 | tf_op jit(solution)/shard_map/pallas_call | solution.py:262
  9.9 0.9 collective-permute-done.refs_0_.refs_6_
  10.8 1.3 %collective-permute-done.1.refs_1_.refs_7_ = bf16[1280,128]{1,0:T(8,128)(2,1)S(1)} collective-permute-done((bf16[1280,128]{1,0:T(8,128)(2,1)S(1)}, bf16[1280,128]{1,0:T(8,128)(2,1)S(1)}, u32[]{:S(2)}, u32[]{:S(2)}) %collective-permute-start.1) | collective-permute-done | bytes 327712 | tf_op jit(solution)/shard_map/ppermute | solution.py:30
  12.1 3.6 %shard_map.75.acc_in = f32[2048,256]{1,0:T(8,128)S(1)} custom-call(s32[32,128]{1,0:T(8,128)S(1)} %get-tuple-element.34.meta_ref, bf16[128,2048]{1,0:T(8,128)(2,1)S(1)} %get-tuple-element.35.q_ref, f32[2,128,128]{2,1,0:T(8,128)S(1)} %get-tuple-element.37.m_ref, bf16[16,128,128]{2,1,0:T(8,128)(2,1)S(1)} %get-tuple-element.38.mask_ref, ...), custom_call_target="tpu_custom_call", output_to_operand_aliasing={{}: (4, {})} | custom-call | flops 1 | bytes 1 | tf_op jit(solution)/shard_map/pallas_call | solution.py:274
  15.7 0.0 collective-permute-done.2.refs_0_.refs_8_
  15.7 5.0 %collective-permute-done.3.refs_1_.refs_9_ = bf16[1280,128]{1,0:T(8,128)(2,1)S(1)} collective-permute-done((bf16[1280,128]{1,0:T(8,128)(2,1)S(1)}, bf16[1280,128]{1,0:T(8,128)(2,1)S(1)}, u32[]{:S(2)}, u32[]{:S(2)}) %collective-permute-start.3) | collective-permute-done | bytes 327712 | tf_op jit(solution)/shard_map/ppermute | solution.py:30
  20.7 0.0 collective-permute-done.4.refs_2_.refs_10_
  20.8 1.3 %collective-permute-start.6 = (bf16[2560,128]{1,0:T(8,128)(2,1)S(1)}, bf16[2560,128]{1,0:T(8,128)(2,1)S(1)}, u32[]{:S(2)}, u32[]{:S(2)}) collective-permute-start(bf16[2560,128]{1,0:T(8,128)(2,1)S(1)} %constant_dynamic-update-slice_fusion), channel_id=1, source_target_pairs={{48,0},{0,16},{16,32},{32,48},{112,64},{64,80},{80,96},{96,112},{1... | collective-permute-start | bytes 1966088 | tf_op jit(solution)/shard_map/ppermute | solution.py:30
  22.1 0.8 collective-permute-start.7
  22.9 1.2 %collective-permute-start.5 = (bf16[1280,128]{1,0:T(8,128)(2,1)S(1)}, bf16[1280,128]{1,0:T(8,128)(2,1)S(1)}, u32[]{:S(2)}, u32[]{:S(2)}) collective-permute-start(bf16[1280,128]{1,0:T(8,128)(2,1)S(1)} %get-tuple-element.47.kv_ref.refs_5_), channel_id=1, source_target_pairs={{128,0},{144,16},{160,32},{176,48},{192,64},{208,80},{224,96},{240... | collective-permute-start | bytes 983048 | tf_op jit(solution)/shard_map/ppermute | solution.py:30
  24.1 2.2 %collective-permute-start.8 = (bf16[1280,128]{1,0:T(8,128)(2,1)S(1)}, bf16[1280,128]{1,0:T(8,128)(2,1)S(1)}, u32[]{:S(2)}, u32[]{:S(2)}) collective-permute-start(bf16[1280,128]{1,0:T(8,128)(2,1)S(1)} %collective-permute-done.4.refs_2_.refs_10_), channel_id=1, source_target_pairs={{192,0},{208,16},{224,32},{240,48},{0,64},{16,80},{32,96},{48,112}... | collective-permute-start | bytes 983048 | tf_op jit(solution)/shard_map/ppermute | solution.py:30
  26.3 0.0 collective-permute-start.9
  26.3 5.3 %shard_map.76.acc_in = f32[2048,256]{1,0:T(8,128)S(1)} custom-call(s32[32,128]{1,0:T(8,128)S(1)} %get-tuple-element.34.meta_ref, bf16[128,2048]{1,0:T(8,128)(2,1)S(1)} %get-tuple-element.35.q_ref, f32[2,128,128]{2,1,0:T(8,128)S(1)} %get-tuple-element.37.m_ref, bf16[16,128,128]{2,1,0:T(8,128)(2,1)S(1)} %get-tuple-element.38.mask_ref, ...), custom_call_target="tpu_custom_call", output_to_operand_aliasing={{}: (4, {})} | custom-call | flops 1 | bytes 1 | tf_op jit(solution)/shard_map/pallas_call | solution.py:274
  31.7 3.5 %collective-permute-done.5.refs_0_.refs_11_ = bf16[1280,128]{1,0:T(8,128)(2,1)S(1)} collective-permute-done((bf16[1280,128]{1,0:T(8,128)(2,1)S(1)}, bf16[1280,128]{1,0:T(8,128)(2,1)S(1)}, u32[]{:S(2)}, u32[]{:S(2)}) %collective-permute-start.5) | collective-permute-done | bytes 327712 | tf_op jit(solution)/shard_map/ppermute | solution.py:30
  35.1 1.2 %collective-permute-start.10 = (bf16[1280,128]{1,0:T(8,128)(2,1)S(1)}, bf16[1280,128]{1,0:T(8,128)(2,1)S(1)}, u32[]{:S(2)}, u32[]{:S(2)}) collective-permute-start(bf16[1280,128]{1,0:T(8,128)(2,1)S(1)} %collective-permute-done.4.refs_2_.refs_10_), channel_id=1, source_target_pairs={{128,0},{144,16},{160,32},{176,48},{192,64},{208,80},{224,96},{240... | collective-permute-start | bytes 983048 | tf_op jit(solution)/shard_map/ppermute | solution.py:30
  36.3 0.0 collective-permute-done.6.refs_1_.refs_12_
  36.3 2.4 %collective-permute-start.11 = (bf16[1280,128]{1,0:T(8,128)(2,1)S(1)}, bf16[1280,128]{1,0:T(8,128)(2,1)S(1)}, u32[]{:S(2)}, u32[]{:S(2)}) collective-permute-start(bf16[1280,128]{1,0:T(8,128)(2,1)S(1)} %collective-permute-done.5.refs_0_.refs_11_), channel_id=1, source_target_pairs={{48,0},{0,16},{16,32},{32,48},{112,64},{64,80},{80,96},{96,112},{1... | collective-permute-start | bytes 983048 | tf_op jit(solution)/shard_map/ppermute | solution.py:30
  38.8 0.0 collective-permute-done.7.refs_2_.refs_13_
  38.8 0.0 collective-permute-start.12
  38.8 8.1 %shard_map.77.acc_in = f32[2048,256]{1,0:T(8,128)S(1)} custom-call(s32[32,128]{1,0:T(8,128)S(1)} %get-tuple-element.34.meta_ref, bf16[128,2048]{1,0:T(8,128)(2,1)S(1)} %get-tuple-element.35.q_ref, f32[2,128,128]{2,1,0:T(8,128)S(1)} %get-tuple-element.37.m_ref, bf16[16,128,128]{2,1,0:T(8,128)(2,1)S(1)} %get-tuple-element.38.mask_ref, ...), custom_call_target="tpu_custom_call", output_to_operand_aliasing={{}: (4, {})} | custom-call | flops 1 | bytes 1 | tf_op jit(solution)/shard_map/pallas_call | solution.py:274
  46.9 0.0 collective-permute-done.8.refs_0_.refs_14_
  46.9 0.0 collective-permute-done.9.refs_1_.refs_15_
  46.9 0.0 collective-permute-done.10.refs_2_.refs_16_
  46.9 0.0 collective-permute-done.11.refs_3_.refs_17_
  46.9 0.1 collective-permute-done.12.refs_4_.refs_18_
  47.1 71.1 %shard_map.78 = bf16[128,2048]{1,0:T(8,128)(2,1)} custom-call(s32[32,128]{1,0:T(8,128)S(1)} %get-tuple-element.34.meta_ref, bf16[128,2048]{1,0:T(8,128)(2,1)S(1)} %get-tuple-element.35.q_ref, f32[2,128,128]{2,1,0:T(8,128)S(1)} %get-tuple-element.37.m_ref, bf16[16,128,128]{2,1,0:T(8,128)(2,1)S(1)} %get-tuple-element.38.mask_ref, ...), custom_call_target="tpu_custom_call" | custom-call | flops 1 | bytes 1 | tf_op jit(solution)/shard_map/pallas_call | solution.py:287
  (2 shorter events, 0.1 us)
Async XLA Ops:
  1.3 9.5 %collective-permute-start = (bf16[1280,128]{1,0:T(8,128)(2,1)S(1)}, bf16[1280,128]{1,0:T(8,128)(2,1)S(1)}, u32[]{:S(2)}, u32[]{:S(2)}) collective-permute-start(bf16[1280,128]{1,0:T(8,128)(2,1)S(1)} %get-tuple-element.47.kv_ref.refs_5_), channel_id=1, source_target_pairs={{192,0},{208,16},{224,32},{240,48},{0,64},{16,80},{32,96},{48,112}... | collective-permute-start | bytes 983048 | tf_op jit(solution)/shard_map/ppermute | solution.py:30
  1.6 10.5 %collective-permute-start.1 = (bf16[1280,128]{1,0:T(8,128)(2,1)S(1)}, bf16[1280,128]{1,0:T(8,128)(2,1)S(1)}, u32[]{:S(2)}, u32[]{:S(2)}) collective-permute-start(bf16[1280,128]{1,0:T(8,128)(2,1)S(1)} %get-tuple-element.47.kv_ref.refs_5_), channel_id=1, source_target_pairs={{64,0},{80,16},{96,32},{112,48},{128,64},{144,80},{160,96},{176,11... | collective-permute-start | bytes 983048 | tf_op jit(solution)/shard_map/ppermute | solution.py:30
  3.4 12.3 %collective-permute-start.2 = (bf16[1280,128]{1,0:T(8,128)(2,1)S(1)}, bf16[1280,128]{1,0:T(8,128)(2,1)S(1)}, u32[]{:S(2)}, u32[]{:S(2)}) collective-permute-start(bf16[1280,128]{1,0:T(8,128)(2,1)S(1)} %get-tuple-element.47.kv_ref.refs_5_), channel_id=1, source_target_pairs={{48,0},{0,16},{16,32},{32,48},{112,64},{64,80},{80,96},{96,112},{1... | collective-permute-start | bytes 983048 | tf_op jit(solution)/shard_map/ppermute | solution.py:30
  3.9 16.8 %collective-permute-start.3 = (bf16[1280,128]{1,0:T(8,128)(2,1)S(1)}, bf16[1280,128]{1,0:T(8,128)(2,1)S(1)}, u32[]{:S(2)}, u32[]{:S(2)}) collective-permute-start(bf16[1280,128]{1,0:T(8,128)(2,1)S(1)} %get-tuple-element.47.kv_ref.refs_5_), channel_id=1, source_target_pairs={{16,0},{32,16},{48,32},{0,48},{80,64},{96,80},{112,96},{64,112},{1... | collective-permute-start | bytes 983048 | tf_op jit(solution)/shard_map/ppermute | solution.py:30
  5.4 15.3 %collective-permute-start.4 = (bf16[1280,128]{1,0:T(8,128)(2,1)S(1)}, bf16[1280,128]{1,0:T(8,128)(2,1)S(1)}, u32[]{:S(2)}, u32[]{:S(2)}) collective-permute-start(bf16[1280,128]{1,0:T(8,128)(2,1)S(1)} %get-tuple-element.47.kv_ref.refs_5_), channel_id=1, source_target_pairs={{32,0},{48,16},{0,32},{16,48},{96,64},{112,80},{64,96},{80,112},{1... | collective-permute-start | bytes 983048 | tf_op jit(solution)/shard_map/ppermute | solution.py:30
  20.8 15.5 %collective-permute-start.6 = (bf16[2560,128]{1,0:T(8,128)(2,1)S(1)}, bf16[2560,128]{1,0:T(8,128)(2,1)S(1)}, u32[]{:S(2)}, u32[]{:S(2)}) collective-permute-start(bf16[2560,128]{1,0:T(8,128)(2,1)S(1)} %constant_dynamic-update-slice_fusion), channel_id=1, source_target_pairs={{48,0},{0,16},{16,32},{32,48},{112,64},{64,80},{80,96},{96,112},{1... | collective-permute-start | bytes 1966088 | tf_op jit(solution)/shard_map/ppermute | solution.py:30
  22.1 16.6 %collective-permute-start.7 = (bf16[2560,128]{1,0:T(8,128)(2,1)S(1)}, bf16[2560,128]{1,0:T(8,128)(2,1)S(1)}, u32[]{:S(2)}, u32[]{:S(2)}) collective-permute-start(bf16[2560,128]{1,0:T(8,128)(2,1)S(1)} %constant_dynamic-update-slice_fusion), channel_id=1, source_target_pairs={{16,0},{32,16},{48,32},{0,48},{80,64},{96,80},{112,96},{64,112},{1... | collective-permute-start | bytes 1966088 | tf_op jit(solution)/shard_map/ppermute | solution.py:30
  22.9 12.2 %collective-permute-start.5 = (bf16[1280,128]{1,0:T(8,128)(2,1)S(1)}, bf16[1280,128]{1,0:T(8,128)(2,1)S(1)}, u32[]{:S(2)}, u32[]{:S(2)}) collective-permute-start(bf16[1280,128]{1,0:T(8,128)(2,1)S(1)} %get-tuple-element.47.kv_ref.refs_5_), channel_id=1, source_target_pairs={{128,0},{144,16},{160,32},{176,48},{192,64},{208,80},{224,96},{240... | collective-permute-start | bytes 983048 | tf_op jit(solution)/shard_map/ppermute | solution.py:30
  24.1 22.8 %collective-permute-start.8 = (bf16[1280,128]{1,0:T(8,128)(2,1)S(1)}, bf16[1280,128]{1,0:T(8,128)(2,1)S(1)}, u32[]{:S(2)}, u32[]{:S(2)}) collective-permute-start(bf16[1280,128]{1,0:T(8,128)(2,1)S(1)} %collective-permute-done.4.refs_2_.refs_10_), channel_id=1, source_target_pairs={{192,0},{208,16},{224,32},{240,48},{0,64},{16,80},{32,96},{48,112}... | collective-permute-start | bytes 983048 | tf_op jit(solution)/shard_map/ppermute | solution.py:30
  26.3 20.6 %collective-permute-start.9 = (bf16[1280,128]{1,0:T(8,128)(2,1)S(1)}, bf16[1280,128]{1,0:T(8,128)(2,1)S(1)}, u32[]{:S(2)}, u32[]{:S(2)}) collective-permute-start(bf16[1280,128]{1,0:T(8,128)(2,1)S(1)} %collective-permute-done.4.refs_2_.refs_10_), channel_id=1, source_target_pairs={{64,0},{80,16},{96,32},{112,48},{128,64},{144,80},{160,96},{176,11... | collective-permute-start | bytes 983048 | tf_op jit(solution)/shard_map/ppermute | solution.py:30
  35.1 11.8 %collective-permute-start.10 = (bf16[1280,128]{1,0:T(8,128)(2,1)S(1)}, bf16[1280,128]{1,0:T(8,128)(2,1)S(1)}, u32[]{:S(2)}, u32[]{:S(2)}) collective-permute-start(bf16[1280,128]{1,0:T(8,128)(2,1)S(1)} %collective-permute-done.4.refs_2_.refs_10_), channel_id=1, source_target_pairs={{128,0},{144,16},{160,32},{176,48},{192,64},{208,80},{224,96},{240... | collective-permute-start | bytes 983048 | tf_op jit(solution)/shard_map/ppermute | solution.py:30
  36.3 10.6 %collective-permute-start.11 = (bf16[1280,128]{1,0:T(8,128)(2,1)S(1)}, bf16[1280,128]{1,0:T(8,128)(2,1)S(1)}, u32[]{:S(2)}, u32[]{:S(2)}) collective-permute-start(bf16[1280,128]{1,0:T(8,128)(2,1)S(1)} %collective-permute-done.5.refs_0_.refs_11_), channel_id=1, source_target_pairs={{48,0},{0,16},{16,32},{32,48},{112,64},{64,80},{80,96},{96,112},{1... | collective-permute-start | bytes 983048 | tf_op jit(solution)/shard_map/ppermute | solution.py:30
  38.8 8.3 %collective-permute-start.12 = (bf16[1280,128]{1,0:T(8,128)(2,1)S(1)}, bf16[1280,128]{1,0:T(8,128)(2,1)S(1)}, u32[]{:S(2)}, u32[]{:S(2)}) collective-permute-start(bf16[1280,128]{1,0:T(8,128)(2,1)S(1)} %collective-permute-done.5.refs_0_.refs_11_), channel_id=1, source_target_pairs={{16,0},{32,16},{48,32},{0,48},{80,64},{96,80},{112,96},{64,112},{1... | collective-permute-start | bytes 983048 | tf_op jit(solution)/shard_map/ppermute | solution.py:30

commit v2 on v1

--- a/solution.py
+++ b/solution.py
@@ -17,8 +17,8 @@
 ORDER = (
     (0, 0),
     (-1, 0), (1, 0), (0, -1), (0, 1), (0, 2),
-    (2, 0), (-1, -1), (1, -1), (-1, 1), (1, 1),
-    (-1, 2), (1, 2), (2, 2), (2, -1), (2, 1),
+    (2, 0), (-1, 2), (1, 2), (-1, -1), (1, -1), (-1, 1), (1, 1),
+    (2, 2), (2, -1), (2, 1),
 )
 
 
@@ -309,26 +309,28 @@
     over_x = from_offset(own, 0, 2)
     acc, peak, mask = begin(own)
 
-    acc, up, down = tie((acc, up, down))
+    acc, up, down, own_later = tie((acc, up, down, own))
+    over_y = from_offset(own_later, 2, 0)
     acc = add(acc, peak, mask, [up, down], 1, 2)
 
-    acc, own_later, up, down, left, right, over_x = tie((acc, own, up, down, left, right, over_x))
+    acc, up, down, left, right, over_x, over_y = tie((acc, up, down, left, right, over_x, over_y))
     column = jnp.concatenate([up, down], 0)
     diag_left, diag_right = from_offset(column, 0, -1), from_offset(column, 0, 1)
-    over_y = from_offset(own_later, 2, 0)
     far_up, far_down = from_offset(over_x, -1, 0), from_offset(over_x, 1, 0)
-    acc = add(acc, peak, mask, [left, right, over_x], 3, 3)
-
-    acc, over_y, over_x_later = tie((acc, over_y, over_x))
-    far_left, far_right = from_offset(over_y, 0, -1), from_offset(over_y, 0, 1)
+    acc = add(acc, peak, mask, [left, right, over_x, over_y], 3, 4)
+
+    acc, far_up, far_down, over_x_later = tie((acc, far_up, far_down, over_x))
     opposite = from_offset(over_x_later, 2, 0)
+    acc = add(acc, peak, mask, [far_up, far_down], 7, 2)
+
     acc, diag_left, diag_right, over_y_later = tie((acc, diag_left, diag_right, over_y))
-    acc = add(acc, peak, mask, [over_y_later, diag_left, diag_right], 6, 5)
-
-    last = [far_up, far_down, opposite, far_left, far_right]
+    far_left, far_right = from_offset(over_y_later, 0, -1), from_offset(over_y_later, 0, 1)
+    acc = add(acc, peak, mask, [diag_left, diag_right], 9, 4)
+
+    last = [opposite, far_left, far_right]
     acc, *last = tie((acc, *last))
-    everything = [own, up, down, left, right, over_x, over_y, diag_left, diag_right]
-    return end(acc, peak, mask, last, 11, 5, everything + last)
+    everything = [own, up, down, left, right, over_x, over_y, far_up, far_down, diag_left, diag_right]
+    return end(acc, peak, mask, last, 13, 3, everything + last)
 
 
 def solution(mesh):

time: 118 us -> 116 us (0.983)
  waiting for transfers between devices: 10.8 us -> 9.55 us
    pallas_call x1, Pallas kernels: 71.1 us -> 68.3 us  [end(): pl.pallas_call(functools.partial(last_kernel, first=first, count=count, p...]
    pallas_call x3 -> x4, Pallas kernels: 17 us -> 19.7 us  [add(): pl.pallas_call(functools.partial(middle_kernel, first=first, count=count,...]
    ppermute x13, waiting for transfers between devices: 10.8 us -> 9.55 us  [from_offset(): return lax.ppermute(block, 'ctx', route)]
  transfers between devices with their start and end apart: 13 -> 13, of which waited for: 5 -> 7; matrix products, arithmetic and copies ran while one was open for 0% -> 0% of each run, Pallas kernels for 17% -> 20%
where the time goes in v2:
time: 116 us
  Pallas kernels  92.4 us (80%)
  starting transfers between devices  13.7 us (12%)
  waiting for transfers between devices  9.55 us (8%)
    pallas_call x1, Pallas kernels, end(): pl.pallas_call(functools.partial(last_kernel, first=first, count=count, p...  68.3 us
    pallas_call x4, Pallas kernels, add(): pl.pallas_call(functools.partial(middle_kernel, first=first, count=count,...  19.7 us
    ppermute x13, starting transfers between devices, from_offset(): return lax.ppermute(block, 'ctx', route)  13.7 us
    ppermute x13, waiting for transfers between devices, from_offset(): return lax.ppermute(block, 'ctx', route)  9.55 us
    pallas_call x1, Pallas kernels, begin(): pl.pallas_call(functools.partial(first_kernel, cached=cached, tokens=toke...  3.1 us
  transfers between devices with their start and end apart: 13, of which 7 were waited for; matrix products, arithmetic and copies ran while one was open for 0% of the time, Pallas kernels for 20%

profile of v2, /device:TPU:62, one launch (start us, length us, event | category | flops | bytes accessed | tf_op | source)
XLA Modules:
  0.0 115.9 jit_solution(9331146804974582848)
XLA Ops:
  0.0 1.3 %shard_map.73 = (bf16[1280,128]{1,0:T(8,128)(2,1)S(1)}, bf16[128,2048]{1,0:T(8,128)(2,1)S(1)}, s32[32,128]{1,0:T(8,128)S(1)}) custom-call(s32[16]{0:T(128)} %lens_ref.1, bf16[512,128]{1,0:T(8,128)(2,1)} %ck_ref.1, bf16[128,128]{1,0:T(8,128)(2,1)} %nk_ref.1, bf16[512,128]{1,0:T(8,128)(2,1)} %cv_ref.1, bf16[128,128]{1,0:T(8,128)(2,1)} %nv_ref.1, ...), custom_call_target="tpu_custom_call" | custom-call | flops 1 | bytes 1 | tf_op jit(solution)/shard_map/pallas_call | solution.py:238
  1.3 0.3 collective-permute-start
  1.6 1.8 %collective-permute-start.1 = (bf16[1280,128]{1,0:T(8,128)(2,1)S(1)}, bf16[1280,128]{1,0:T(8,128)(2,1)S(1)}, u32[]{:S(2)}, u32[]{:S(2)}) collective-permute-start(bf16[1280,128]{1,0:T(8,128)(2,1)S(1)} %get-tuple-element.43.kv_ref.refs_3_), channel_id=1, source_target_pairs={{64,0},{80,16},{96,32},{112,48},{128,64},{144,80},{160,96},{176,11... | collective-permute-start | bytes 983048 | tf_op jit(solution)/shard_map/ppermute | solution.py:30
  3.4 0.5 collective-permute-start.2
  3.9 1.5 %collective-permute-start.3 = (bf16[1280,128]{1,0:T(8,128)(2,1)S(1)}, bf16[1280,128]{1,0:T(8,128)(2,1)S(1)}, u32[]{:S(2)}, u32[]{:S(2)}) collective-permute-start(bf16[1280,128]{1,0:T(8,128)(2,1)S(1)} %get-tuple-element.43.kv_ref.refs_3_), channel_id=1, source_target_pairs={{16,0},{32,16},{48,32},{0,48},{80,64},{96,80},{112,96},{64,112},{1... | collective-permute-start | bytes 983048 | tf_op jit(solution)/shard_map/ppermute | solution.py:30
  5.4 1.4 %collective-permute-start.4 = (bf16[1280,128]{1,0:T(8,128)(2,1)S(1)}, bf16[1280,128]{1,0:T(8,128)(2,1)S(1)}, u32[]{:S(2)}, u32[]{:S(2)}) collective-permute-start(bf16[1280,128]{1,0:T(8,128)(2,1)S(1)} %get-tuple-element.43.kv_ref.refs_3_), channel_id=1, source_target_pairs={{32,0},{48,16},{0,32},{16,48},{96,64},{112,80},{64,96},{80,112},{1... | collective-permute-start | bytes 983048 | tf_op jit(solution)/shard_map/ppermute | solution.py:30
  6.8 3.1 %shard_map.74 = (f32[2048,256]{1,0:T(8,128)S(1)}, f32[2,128,128]{2,1,0:T(8,128)S(1)}, bf16[16,128,128]{2,1,0:T(8,128)(2,1)S(1)}) custom-call(bf16[128,2048]{1,0:T(8,128)(2,1)S(1)} %get-tuple-element.35.q_ref, s32[32,128]{1,0:T(8,128)S(1)} %get-tuple-element.34.meta_ref, bf16[1280,128]{1,0:T(8,128)(2,1)S(1)} %get-tuple-element.43.kv_ref.refs_3_), custom_call_target="tpu_custom_call" | custom-call | flops 1 | bytes 1 | tf_op jit(solution)/shard_map/pallas_call | solution.py:262
  9.9 0.9 collective-permute-done.refs_0_.refs_4_
  10.8 1.3 %collective-permute-done.1.refs_1_.refs_5_ = bf16[1280,128]{1,0:T(8,128)(2,1)S(1)} collective-permute-done((bf16[1280,128]{1,0:T(8,128)(2,1)S(1)}, bf16[1280,128]{1,0:T(8,128)(2,1)S(1)}, u32[]{:S(2)}, u32[]{:S(2)}) %collective-permute-start.1) | collective-permute-done | bytes 327712 | tf_op jit(solution)/shard_map/ppermute | solution.py:30
  12.1 1.2 %collective-permute-start.5 = (bf16[1280,128]{1,0:T(8,128)(2,1)S(1)}, bf16[1280,128]{1,0:T(8,128)(2,1)S(1)}, u32[]{:S(2)}, u32[]{:S(2)}) collective-permute-start(bf16[1280,128]{1,0:T(8,128)(2,1)S(1)} %get-tuple-element.43.kv_ref.refs_3_), channel_id=1, source_target_pairs={{128,0},{144,16},{160,32},{176,48},{192,64},{208,80},{224,96},{240... | collective-permute-start | bytes 983048 | tf_op jit(solution)/shard_map/ppermute | solution.py:30
  13.4 3.6 %shard_map.75.acc_in = f32[2048,256]{1,0:T(8,128)S(1)} custom-call(s32[32,128]{1,0:T(8,128)S(1)} %get-tuple-element.34.meta_ref, bf16[128,2048]{1,0:T(8,128)(2,1)S(1)} %get-tuple-element.35.q_ref, f32[2,128,128]{2,1,0:T(8,128)S(1)} %get-tuple-element.37.m_ref, bf16[16,128,128]{2,1,0:T(8,128)(2,1)S(1)} %get-tuple-element.38.mask_ref, ...), custom_call_target="tpu_custom_call", output_to_operand_aliasing={{}: (4, {})} | custom-call | flops 1 | bytes 1 | tf_op jit(solution)/shard_map/pallas_call | solution.py:274
  17.0 0.0 collective-permute-done.2.refs_0_.refs_6_
  17.0 3.8 %collective-permute-done.3.refs_1_.refs_7_ = bf16[1280,128]{1,0:T(8,128)(2,1)S(1)} collective-permute-done((bf16[1280,128]{1,0:T(8,128)(2,1)S(1)}, bf16[1280,128]{1,0:T(8,128)(2,1)S(1)}, u32[]{:S(2)}, u32[]{:S(2)}) %collective-permute-start.3) | collective-permute-done | bytes 327712 | tf_op jit(solution)/shard_map/ppermute | solution.py:30
  20.7 0.0 collective-permute-done.4.refs_2_.refs_8_
  20.7 1.3 %collective-permute-done.5.refs_3_.refs_9_ = bf16[1280,128]{1,0:T(8,128)(2,1)S(1)} collective-permute-done((bf16[1280,128]{1,0:T(8,128)(2,1)S(1)}, bf16[1280,128]{1,0:T(8,128)(2,1)S(1)}, u32[]{:S(2)}, u32[]{:S(2)}) %collective-permute-start.5) | collective-permute-done | bytes 327712 | tf_op jit(solution)/shard_map/ppermute | solution.py:30
  22.1 0.6 collective-permute-start.8
  22.7 1.5 %collective-permute-start.9 = (bf16[2560,128]{1,0:T(8,128)(2,1)S(1)}, bf16[2560,128]{1,0:T(8,128)(2,1)S(1)}, u32[]{:S(2)}, u32[]{:S(2)}) collective-permute-start(bf16[2560,128]{1,0:T(8,128)(2,1)S(1)} %constant_dynamic-update-slice_fusion), channel_id=1, source_target_pairs={{16,0},{32,16},{48,32},{0,48},{80,64},{96,80},{112,96},{64,112},{1... | collective-permute-start | bytes 1966088 | tf_op jit(solution)/shard_map/ppermute | solution.py:30
  24.2 0.4 collective-permute-start.6
  24.7 1.6 %collective-permute-start.7 = (bf16[1280,128]{1,0:T(8,128)(2,1)S(1)}, bf16[1280,128]{1,0:T(8,128)(2,1)S(1)}, u32[]{:S(2)}, u32[]{:S(2)}) collective-permute-start(bf16[1280,128]{1,0:T(8,128)(2,1)S(1)} %collective-permute-done.4.refs_2_.refs_8_), channel_id=1, source_target_pairs={{64,0},{80,16},{96,32},{112,48},{128,64},{144,80},{160,96},{176,11... | collective-permute-start | bytes 983048 | tf_op jit(solution)/shard_map/ppermute | solution.py:30
  26.3 6.2 %shard_map.76.acc_in = f32[2048,256]{1,0:T(8,128)S(1)} custom-call(s32[32,128]{1,0:T(8,128)S(1)} %get-tuple-element.34.meta_ref, bf16[128,2048]{1,0:T(8,128)(2,1)S(1)} %get-tuple-element.35.q_ref, f32[2,128,128]{2,1,0:T(8,128)S(1)} %get-tuple-element.37.m_ref, bf16[16,128,128]{2,1,0:T(8,128)(2,1)S(1)} %get-tuple-element.38.mask_ref, ...), custom_call_target="tpu_custom_call", output_to_operand_aliasing={{}: (4, {})} | custom-call | flops 1 | bytes 1 | tf_op jit(solution)/shard_map/pallas_call | solution.py:274
  32.5 0.0 collective-permute-done.6.refs_0_.refs_10_
  32.5 0.4 collective-permute-done.7.refs_1_.refs_11_
  33.0 0.7 collective-permute-start.10
  33.7 3.6 %shard_map.77.acc_in = f32[2048,256]{1,0:T(8,128)S(1)} custom-call(s32[32,128]{1,0:T(8,128)S(1)} %get-tuple-element.34.meta_ref, bf16[128,2048]{1,0:T(8,128)(2,1)S(1)} %get-tuple-element.35.q_ref, f32[2,128,128]{2,1,0:T(8,128)S(1)} %get-tuple-element.37.m_ref, bf16[16,128,128]{2,1,0:T(8,128)(2,1)S(1)} %get-tuple-element.38.mask_ref, ...), custom_call_target="tpu_custom_call", output_to_operand_aliasing={{}: (4, {})} | custom-call | flops 1 | bytes 1 | tf_op jit(solution)/shard_map/pallas_call | solution.py:274
  37.3 0.0 collective-permute-done.8.refs_0_.refs_12_
  37.3 0.8 collective-permute-done.9.refs_1_.refs_13_
  38.1 1.0 collective-permute-start.11
  39.2 1.0 collective-permute-start.12
  40.2 6.2 %shard_map.78.acc_in = f32[2048,256]{1,0:T(8,128)S(1)} custom-call(s32[32,128]{1,0:T(8,128)S(1)} %get-tuple-element.34.meta_ref, bf16[128,2048]{1,0:T(8,128)(2,1)S(1)} %get-tuple-element.35.q_ref, f32[2,128,128]{2,1,0:T(8,128)S(1)} %get-tuple-element.37.m_ref, bf16[16,128,128]{2,1,0:T(8,128)(2,1)S(1)} %get-tuple-element.38.mask_ref, ...), custom_call_target="tpu_custom_call", output_to_operand_aliasing={{}: (4, {})} | custom-call | flops 1 | bytes 1 | tf_op jit(solution)/shard_map/pallas_call | solution.py:274
  46.4 0.0 collective-permute-done.10.refs_0_.refs_14_
  46.4 1.0 collective-permute-done.12.refs_2_.refs_16_
  47.4 68.3 %shard_map.79 = bf16[128,2048]{1,0:T(8,128)(2,1)} custom-call(s32[32,128]{1,0:T(8,128)S(1)} %get-tuple-element.34.meta_ref, bf16[128,2048]{1,0:T(8,128)(2,1)S(1)} %get-tuple-element.35.q_ref, f32[2,128,128]{2,1,0:T(8,128)S(1)} %get-tuple-element.37.m_ref, bf16[16,128,128]{2,1,0:T(8,128)(2,1)S(1)} %get-tuple-element.38.mask_ref, ...), custom_call_target="tpu_custom_call" | custom-call | flops 1 | bytes 1 | tf_op jit(solution)/shard_map/pallas_call | solution.py:287
  (3 shorter events, 0.1 us)
Async XLA Ops:
  1.3 9.5 %collective-permute-start = (bf16[1280,128]{1,0:T(8,128)(2,1)S(1)}, bf16[1280,128]{1,0:T(8,128)(2,1)S(1)}, u32[]{:S(2)}, u32[]{:S(2)}) collective-permute-start(bf16[1280,128]{1,0:T(8,128)(2,1)S(1)} %get-tuple-element.43.kv_ref.refs_3_), channel_id=1, source_target_pairs={{192,0},{208,16},{224,32},{240,48},{0,64},{16,80},{32,96},{48,112}... | collective-permute-start | bytes 983048 | tf_op jit(solution)/shard_map/ppermute | solution.py:30
  1.6 10.5 %collective-permute-start.1 = (bf16[1280,128]{1,0:T(8,128)(2,1)S(1)}, bf16[1280,128]{1,0:T(8,128)(2,1)S(1)}, u32[]{:S(2)}, u32[]{:S(2)}) collective-permute-start(bf16[1280,128]{1,0:T(8,128)(2,1)S(1)} %get-tuple-element.43.kv_ref.refs_3_), channel_id=1, source_target_pairs={{64,0},{80,16},{96,32},{112,48},{128,64},{144,80},{160,96},{176,11... | collective-permute-start | bytes 983048 | tf_op jit(solution)/shard_map/ppermute | solution.py:30
  3.4 13.6 %collective-permute-start.2 = (bf16[1280,128]{1,0:T(8,128)(2,1)S(1)}, bf16[1280,128]{1,0:T(8,128)(2,1)S(1)}, u32[]{:S(2)}, u32[]{:S(2)}) collective-permute-start(bf16[1280,128]{1,0:T(8,128)(2,1)S(1)} %get-tuple-element.43.kv_ref.refs_3_), channel_id=1, source_target_pairs={{48,0},{0,16},{16,32},{32,48},{112,64},{64,80},{80,96},{96,112},{1... | collective-permute-start | bytes 983048 | tf_op jit(solution)/shard_map/ppermute | solution.py:30
  3.9 16.8 %collective-permute-start.3 = (bf16[1280,128]{1,0:T(8,128)(2,1)S(1)}, bf16[1280,128]{1,0:T(8,128)(2,1)S(1)}, u32[]{:S(2)}, u32[]{:S(2)}) collective-permute-start(bf16[1280,128]{1,0:T(8,128)(2,1)S(1)} %get-tuple-element.43.kv_ref.refs_3_), channel_id=1, source_target_pairs={{16,0},{32,16},{48,32},{0,48},{80,64},{96,80},{112,96},{64,112},{1... | collective-permute-start | bytes 983048 | tf_op jit(solution)/shard_map/ppermute | solution.py:30
  5.4 15.3 %collective-permute-start.4 = (bf16[1280,128]{1,0:T(8,128)(2,1)S(1)}, bf16[1280,128]{1,0:T(8,128)(2,1)S(1)}, u32[]{:S(2)}, u32[]{:S(2)}) collective-permute-start(bf16[1280,128]{1,0:T(8,128)(2,1)S(1)} %get-tuple-element.43.kv_ref.refs_3_), channel_id=1, source_target_pairs={{32,0},{48,16},{0,32},{16,48},{96,64},{112,80},{64,96},{80,112},{1... | collective-permute-start | bytes 983048 | tf_op jit(solution)/shard_map/ppermute | solution.py:30
  12.1 9.9 %collective-permute-start.5 = (bf16[1280,128]{1,0:T(8,128)(2,1)S(1)}, bf16[1280,128]{1,0:T(8,128)(2,1)S(1)}, u32[]{:S(2)}, u32[]{:S(2)}) collective-permute-start(bf16[1280,128]{1,0:T(8,128)(2,1)S(1)} %get-tuple-element.43.kv_ref.refs_3_), channel_id=1, source_target_pairs={{128,0},{144,16},{160,32},{176,48},{192,64},{208,80},{224,96},{240... | collective-permute-start | bytes 983048 | tf_op jit(solution)/shard_map/ppermute | solution.py:30
  22.1 15.2 %collective-permute-start.8 = (bf16[2560,128]{1,0:T(8,128)(2,1)S(1)}, bf16[2560,128]{1,0:T(8,128)(2,1)S(1)}, u32[]{:S(2)}, u32[]{:S(2)}) collective-permute-start(bf16[2560,128]{1,0:T(8,128)(2,1)S(1)} %constant_dynamic-update-slice_fusion), channel_id=1, source_target_pairs={{48,0},{0,16},{16,32},{32,48},{112,64},{64,80},{80,96},{96,112},{1... | collective-permute-start | bytes 1966088 | tf_op jit(solution)/shard_map/ppermute | solution.py:30
  22.7 15.5 %collective-permute-start.9 = (bf16[2560,128]{1,0:T(8,128)(2,1)S(1)}, bf16[2560,128]{1,0:T(8,128)(2,1)S(1)}, u32[]{:S(2)}, u32[]{:S(2)}) collective-permute-start(bf16[2560,128]{1,0:T(8,128)(2,1)S(1)} %constant_dynamic-update-slice_fusion), channel_id=1, source_target_pairs={{16,0},{32,16},{48,32},{0,48},{80,64},{96,80},{112,96},{64,112},{1... | collective-permute-start | bytes 1966088 | tf_op jit(solution)/shard_map/ppermute | solution.py:30
  24.2 8.3 %collective-permute-start.6 = (bf16[1280,128]{1,0:T(8,128)(2,1)S(1)}, bf16[1280,128]{1,0:T(8,128)(2,1)S(1)}, u32[]{:S(2)}, u32[]{:S(2)}) collective-permute-start(bf16[1280,128]{1,0:T(8,128)(2,1)S(1)} %collective-permute-done.4.refs_2_.refs_8_), channel_id=1, source_target_pairs={{192,0},{208,16},{224,32},{240,48},{0,64},{16,80},{32,96},{48,112}... | collective-permute-start | bytes 983048 | tf_op jit(solution)/shard_map/ppermute | solution.py:30
  24.7 8.3 %collective-permute-start.7 = (bf16[1280,128]{1,0:T(8,128)(2,1)S(1)}, bf16[1280,128]{1,0:T(8,128)(2,1)S(1)}, u32[]{:S(2)}, u32[]{:S(2)}) collective-permute-start(bf16[1280,128]{1,0:T(8,128)(2,1)S(1)} %collective-permute-done.4.refs_2_.refs_8_), channel_id=1, source_target_pairs={{64,0},{80,16},{96,32},{112,48},{128,64},{144,80},{160,96},{176,11... | collective-permute-start | bytes 983048 | tf_op jit(solution)/shard_map/ppermute | solution.py:30
  33.0 13.5 %collective-permute-start.10 = (bf16[1280,128]{1,0:T(8,128)(2,1)S(1)}, bf16[1280,128]{1,0:T(8,128)(2,1)S(1)}, u32[]{:S(2)}, u32[]{:S(2)}) collective-permute-start(bf16[1280,128]{1,0:T(8,128)(2,1)S(1)} %collective-permute-done.4.refs_2_.refs_8_), channel_id=1, source_target_pairs={{128,0},{144,16},{160,32},{176,48},{192,64},{208,80},{224,96},{240... | collective-permute-start | bytes 983048 | tf_op jit(solution)/shard_map/ppermute | solution.py:30
  38.1 8.3 %collective-permute-start.11 = (bf16[1280,128]{1,0:T(8,128)(2,1)S(1)}, bf16[1280,128]{1,0:T(8,128)(2,1)S(1)}, u32[]{:S(2)}, u32[]{:S(2)}) collective-permute-start(bf16[1280,128]{1,0:T(8,128)(2,1)S(1)} %collective-permute-done.5.refs_3_.refs_9_), channel_id=1, source_target_pairs={{48,0},{0,16},{16,32},{32,48},{112,64},{64,80},{80,96},{96,112},{1... | collective-permute-start | bytes 983048 | tf_op jit(solution)/shard_map/ppermute | solution.py:30
  39.2 8.3 %collective-permute-start.12 = (bf16[1280,128]{1,0:T(8,128)(2,1)S(1)}, bf16[1280,128]{1,0:T(8,128)(2,1)S(1)}, u32[]{:S(2)}, u32[]{:S(2)}) collective-permute-start(bf16[1280,128]{1,0:T(8,128)(2,1)S(1)} %collective-permute-done.5.refs_3_.refs_9_), channel_id=1, source_target_pairs={{16,0},{32,16},{48,32},{0,48},{80,64},{96,80},{112,96},{64,112},{1... | collective-permute-start | bytes 983048 | tf_op jit(solution)/shard_map/ppermute | solution.py:30
